TPU v7x, 32 devices: a whole 2x2x4 slice. The times are simulated.
32 devices in a mesh: row: 16 (over z, x, core), rhs: 2 (over y).
Axes of the slice: x: 2, y: 2, z: 4, core: 2. Of those that a mesh axis runs over, the one named last changes fastest.
Arguments:
- rhs_in: float32 [2, 128, 8192], P(None, ('rhs', 'row')), may hold values from -6 to 6
- pivots: int32 [8192], replicated, may hold values from 0 to 8191, each once
- owners: int32 [16], replicated, may hold values from 0 to 15, each once
- panel_first: float32 [2, 8192, 512], P(None, 'row'), may hold values from -0.1875 to 0.1875
- panel_second: float32 [2, 8192, 512], P(None, 'row'), may hold values from -0.1875 to 0.1875
- inverse_first: float32 [2, 512, 512], replicated, may hold values from -0.1875 to 0.1875
- inverse_second: float32 [2, 512, 512], replicated, may hold values from -0.1875 to 0.1875
Outputs:
- solved_rhs: float32 [2, 128, 8192], P(None, 'rhs', 'row')
Inputs may be any that keep to these rules, and one draw needn't show every extreme that they name: `pivots`: each row number occurs once. `owners`: each device index along row occurs once.
All inputs are finite; a program needn't handle non-finite values.
Results may differ from a plain program's by a relative error of at most 0.0001.
Values sent between devices are 32-bit elements; how exact they have to be, the bound alone decides.
A program may use at most 128 MiB of HBM per device.

v0:
```python
import functools

import jax
import jax.numpy as jnp
from jax import lax
from jax.experimental import pallas as pl
from jax.experimental.pallas import tpu as pltpu
from jax.sharding import PartitionSpec as P

LANES = 128
SHIFT = 8
WIDTH = 1 << SHIFT
MESH = pl.DeviceIdType.MESH


def split_matrix(matrix, high, low):
    depth = matrix.shape[2]
    for part in range(2):
        columns = slice(part * depth, (part + 1) * depth)
        values = matrix[part]
        rounded = values.astype(jnp.bfloat16)
        high[:, columns] = rounded
        low[:, columns] = (values - rounded.astype(jnp.float32)).astype(jnp.bfloat16)


def complex_product(operand, high, low):
    groups, size, depth = operand.shape
    half = size // 2
    swapped = pltpu.roll(operand, half, axis=1)
    is_real = lax.broadcasted_iota(jnp.int32, operand.shape, 1) < half
    swapped = jnp.where(is_real, -swapped, swapped)
    rows = groups * size
    wide = jnp.concatenate(
        [operand.reshape(rows, depth), swapped.reshape(rows, depth)], axis=1
    )
    top = wide.astype(jnp.bfloat16).astype(jnp.float32)
    both = jnp.concatenate([top, wide - top], axis=0).astype(jnp.bfloat16)
    contract = (((1,), (1,)), ((), ()))
    main = lax.dot_general(both, high[...], contract, preferred_element_type=jnp.float32)
    first = both[:rows] if rows % 16 == 0 else both
    rest = lax.dot_general(first, low[...], contract, preferred_element_type=jnp.float32)
    return (main[:rows] + main[rows:] + rest[:rows]).reshape(groups, size, depth)


def kernel(
    axis,
    count,
    owners_in,
    pivots_in,
    rhs_in,
    panel_first,
    panel_second,
    inverse_first,
    inverse_second,
    out,
    owners,
    pivots,
    raw,
    values,
    table,
    permuted,
    current,
    updated,
    product,
    block_one,
    merged,
    from_sibling,
    returned,
    solution_zero,
    solution_one,
    factors,
    high,
    low,
    load_sem,
    send_sem,
    receive_sem,
):
    me = lax.axis_index(axis)
    half = raw.shape[1]
    length = raw.shape[2]
    block_size = permuted.shape[2]
    tiles = block_size // LANES
    pairs = count // 2
    chip = lax.div(me, 2)
    core = lax.rem(me, 2)
    sibling = me + 1 - 2 * core
    middle = pairs // 2
    side = lax.div(chip, middle)
    own_slot = core * pairs + chip

    loads = [pltpu.make_async_copy(rhs_in, raw, load_sem.at[4])]
    for place, source in enumerate((inverse_first, panel_first, inverse_second, panel_second)):
        loads.append(pltpu.make_async_copy(source, factors.at[place], load_sem.at[place]))
    small = [
        pltpu.make_async_copy(owners_in, owners, load_sem.at[5]),
        pltpu.make_async_copy(pivots_in, pivots, load_sem.at[6]),
    ]
    for load in small + loads[:2]:
        load.start()

    def each_chip(body):
        @pl.loop(0, middle)
        def _(step):
            body((1 - side) * middle + lax.rem(chip + step, middle))

        @pl.loop(1, middle)
        def _(step):
            body(side * middle + lax.rem(chip + step, middle))

    def each_chip_near_first(body):
        @pl.loop(1, middle)
        def _(step):
            body(side * middle + lax.rem(chip + step, middle))

        @pl.loop(0, middle)
        def _(step):
            body((1 - side) * middle + lax.rem(chip + step, middle))

    barrier = pltpu.get_barrier_semaphore()

    @pl.loop(1, count)
    def _(step):
        pl.semaphore_signal(
            barrier,
            inc=1,
            device_id={axis: lax.rem(me + step, count)},
            device_id_type=MESH,
        )

    def remote(phase, source, target, peer, send_slot, receive_slot):
        return pltpu.make_async_remote_copy(
            src_ref=source,
            dst_ref=target,
            send_sem=send_sem.at[phase, send_slot],
            recv_sem=receive_sem.at[phase, receive_slot],
            device_id={axis: peer},
            device_id_type=MESH,
        )

    def spread(phase, chunks):
        def direct(other):
            return remote(
                phase, chunks.at[own_slot], chunks.at[own_slot], 2 * other + core, other, own_slot
            )

        def relay(other):
            slot = core * pairs + other
            return remote(phase, chunks.at[slot], chunks.at[slot], sibling, pairs + other, slot)

        def begin():
            each_chip(lambda other: direct(other).start())
            relay(chip).start()

        def forward():
            def one(other):
                slot = core * pairs + other
                remote(
                    phase, chunks.at[slot], chunks.at[slot], 2 * other + core, other, slot
                ).wait_recv()
                relay(other).start()

            each_chip_near_first(one)

        def complete():
            @pl.loop(0, pairs)
            def _(other):
                slot = (1 - core) * pairs + other
                remote(
                    phase, chunks.at[slot], chunks.at[slot], sibling, pairs + other, slot
                ).wait_recv()

        def drain():
            each_chip(lambda other: direct(other).wait_send())

            @pl.loop(0, pairs)
            def _(other):
                relay(other).wait_send()

        return begin, forward, complete, drain

    def deal(target_chip, target_core):
        slot = target_core * pairs + target_chip
        return remote(
            2,
            permuted.at[slot],
            current.at[own_slot],
            2 * target_chip + target_core,
            slot,
            own_slot,
        )

    def hand_back(other):
        return remote(
            3, merged.at[other], returned.at[chip], 2 * other + core, other, chip
        )

    def pair_copy():
        return remote(
            3,
            product.at[pl.ds((1 - core) * pairs, pairs)],
            from_sibling,
            sibling,
            pairs,
            pairs,
        )

    def block_at(slot):
        block = jnp.int32(0)
        for j in range(count):
            block = jnp.where(owners[j] == slot, j, block)
        return block

    def gather(block):
        groups = length // WIDTH
        index = [pivots[pl.ds(block * tiles + t, 1), :] for t in range(tiles)]
        index = jnp.concatenate(index, axis=1)
        column = jnp.broadcast_to(index & (WIDTH - 1), (WIDTH, block_size))
        place = lax.broadcasted_iota(jnp.int32, (WIDTH, block_size), 0)
        chosen = jnp.where(column == place, 1.0, 0.0).astype(jnp.bfloat16)
        found = jnp.dot(table[...], chosen, preferred_element_type=jnp.float32)
        group = jnp.broadcast_to(lax.shift_right_logical(index, SHIFT), (2 * half, block_size))
        taken = jnp.zeros((2 * half, block_size), jnp.float32)
        for g in range(groups):
            top = found[g * 2 * half : (g + 1) * 2 * half]
            rest = found[(groups + g) * 2 * half : (groups + g + 1) * 2 * half]
            taken = jnp.where(group == g, top + rest, taken)
        return taken

    def prepare(place):
        loads[place + 1].wait()
        split_matrix(factors.at[place], high.at[place], low.at[place])

    def gather_pair(target_chip):
        for target_core in range(2):
            chunk = gather(block_at(2 * target_chip + target_core))
            permuted[target_core * pairs + target_chip] = chunk

    def deal_chip(step):
        near = lax.div(step, middle)
        target_side = (1 - side) * (1 - near) + side * near
        target_chip = target_side * middle + lax.rem(chip + 1 + step, middle)
        gather_pair(target_chip)
        for target_core in range(2):
            deal(target_chip, target_core).start()

    begin_zero, forward_zero, complete_zero, drain_zero = spread(0, solution_zero)
    begin_one, forward_one, complete_one, drain_one = spread(1, solution_one)

    for load in small:
        load.wait()
    loads[0].wait()
    groups = length // WIDTH
    for g in range(groups):
        columns = slice(g * WIDTH, (g + 1) * WIDTH)
        wide = jnp.concatenate([raw[0, :, columns], raw[1, :, columns]], axis=0)
        values[g * 2 * half : (g + 1) * 2 * half, :] = wide
    rounded = values[...].astype(jnp.bfloat16)
    rows = groups * 2 * half
    table[:rows] = rounded
    table[rows:] = (values[...] - rounded.astype(jnp.float32)).astype(jnp.bfloat16)
    prepare(0)
    for load in loads[2:]:
        load.start()
    solution_zero[own_slot] = complex_product(gather(0)[None], high.at[0], low.at[0])[0]
    pl.semaphore_wait(barrier, count - 1)
    begin_zero()

    @pl.loop(0, middle)
    def _(step):
        deal_chip(step)

    prepare(1)
    forward_zero()
    block_one[...] = gather(1)

    complete_zero()
    product[...] = complex_product(solution_zero[...], high.at[1], low.at[1])
    pair_copy().start()
    deal_chip(middle)
    pair_copy().wait_recv()
    mine = product[pl.ds(core * pairs, pairs)]
    theirs = jnp.full(mine.shape, block_at(sibling), jnp.int32) == 1
    merged[...] = jnp.where(theirs, from_sibling[...], mine)
    each_chip(lambda other: hand_back(other).start())
    returned[chip] = merged[chip]

    @pl.loop(middle + 1, pairs - 1)
    def _(step):
        deal_chip(step)

    prepare(2)
    gather_pair(chip)
    deal(chip, 1 - core).start()
    current[own_slot] = permuted[own_slot]
    my_block = block_at(me)

    @pl.loop(1, pairs)
    def _(step):
        other = lax.rem(chip + step, pairs)
        remote(3, returned.at[other], returned.at[other], sibling, other, other).wait_recv()

    second = block_one[...] - returned[lax.div(owners[1], 2)]
    solution_one[own_slot] = complex_product(second[None], high.at[2], low.at[2])[0]
    begin_one()

    @pl.loop(1, count)
    def _(step):
        slot = lax.rem(own_slot + step, count)
        remote(2, current.at[slot], current.at[slot], sibling, slot, slot).wait_recv()

    before = current[...]
    block = jnp.full(before.shape, my_block, jnp.int32)
    updated[...] = jnp.where(block > 0, before - product[...], solution_zero[...])
    prepare(3)
    forward_one()
    drain_zero()
    pair_copy().wait_send()
    each_chip(lambda other: hand_back(other).wait_send())

    @pl.loop(1, count)
    def _(step):
        slot = lax.rem(own_slot + step, count)
        deal(lax.rem(slot, pairs), lax.div(slot, pairs)).wait_send()

    def last_half(first):
        rows = pl.ds(first, pairs)
        one = solution_one[rows]
        before = updated[rows]
        block = jnp.full(before.shape, my_block, jnp.int32)
        after = before - complex_product(one, high.at[3], low.at[3])
        current[rows] = jnp.where(block > 1, after, jnp.where(block == 1, one, before))

    last_half(core * pairs)
    complete_one()
    last_half((1 - core) * pairs)
    for part in range(2):
        rows = slice(part * half, (part + 1) * half)
        both = [current[c * pairs : (c + 1) * pairs, rows, :] for c in range(2)]
        out[part] = jnp.concatenate(both, axis=1).reshape(count * half, block_size)

    drain_one()


def shards(rhs_in, pivots, owners, panel_first, panel_second, inverse_first, inverse_second, *, count):
    parts, half, length = rhs_in.shape
    block_size = panel_first.shape[2]
    chunks = (count, parts * half, block_size)
    part_chunks = (count // 2, parts * half, block_size)
    return pl.pallas_call(
        functools.partial(kernel, "row", count),
        out_shape=jax.ShapeDtypeStruct((parts, count * half, block_size), jnp.float32),
        in_specs=[pl.BlockSpec(memory_space=pltpu.HBM)] * 7,
        out_specs=pl.BlockSpec(memory_space=pltpu.VMEM),
        scratch_shapes=[
            pltpu.SMEM((count,), jnp.int32),
            pltpu.VMEM((length // LANES, LANES), jnp.int32),
            pltpu.VMEM((parts, half, length), jnp.float32),
            pltpu.VMEM((parts * half * length // WIDTH, WIDTH), jnp.float32),
            pltpu.VMEM((2 * parts * half * length // WIDTH, WIDTH), jnp.bfloat16),
            pltpu.VMEM(chunks, jnp.float32),
            pltpu.VMEM(chunks, jnp.float32),
            pltpu.VMEM(chunks, jnp.float32),
            pltpu.VMEM(chunks, jnp.float32),
            pltpu.VMEM(chunks[1:], jnp.float32),
            pltpu.VMEM(part_chunks, jnp.float32),
            pltpu.VMEM(part_chunks, jnp.float32),
            pltpu.VMEM(part_chunks, jnp.float32),
            pltpu.VMEM(chunks, jnp.float32),
            pltpu.VMEM(chunks, jnp.float32),
            pltpu.VMEM((4, parts, block_size, block_size), jnp.float32),
            pltpu.VMEM((4, block_size, parts * block_size), jnp.bfloat16),
            pltpu.VMEM((4, block_size, parts * block_size), jnp.bfloat16),
            pltpu.SemaphoreType.DMA((7,)),
            pltpu.SemaphoreType.DMA((4, count)),
            pltpu.SemaphoreType.DMA((4, count)),
        ],
        compiler_params=pltpu.CompilerParams(
            collective_id=0, has_side_effects=True, vmem_limit_bytes=57 * 1024 * 1024
        ),
        cost_estimate=pl.CostEstimate(flops=4 * 10**9, bytes_accessed=9 * 10**6, transcendentals=0),
    )(
        owners,
        pivots.reshape(length // LANES, LANES),
        rhs_in,
        panel_first,
        panel_second,
        inverse_first,
        inverse_second,
    )


def solution(mesh):
    return jax.shard_map(
        functools.partial(shards, count=mesh.shape["row"]),
        mesh=mesh,
        in_specs=(
            P(None, ("rhs", "row"), None),
            P(),
            P(),
            P(None, "row", None),
            P(None, "row", None),
            P(),
            P(),
        ),
        out_specs=P(None, "rhs", "row"),
        check_vma=False,
    )
```

profile of v0, /device:TPU:0, one launch (start us, length us, event | category | flops | bytes accessed | tf_op | source)
XLA Modules:
  0.0 33.4 jit_solution(16766368505668156167)
XLA Ops:
  0.0 31.8 %shard_map.73 = f32[2,64,512]{2,1,0:T(8,128)} custom-call(s32[16]{0:T(128)} %owners_in.1, s32[64,128]{1,0:T(8,128)} %bitcast.1, f32[2,4,8192]{2,1,0:T(4,128)} %rhs_in.1, f32[2,512,512]{2,1,0:T(8,128)} %panel_first.1, f32[2,512,512]{2,1,0:T(8,128)} %panel_second.1, f32[2,512,512]{2,1,0:T(8,128)} %inverse_first.1, f32[2,512,512]{2,1,0:T(8,128)} %inverse_second.1), custom_call_target="tpu_custom_call" | custom-call | flops 4000000000 | bytes 9000000 | tf_op jit(solution)/shard_map/pallas_call | solution.py:349
  31.8 1.7 %copy.9 = f32[2,64,512]{2,1,0:T(8,128)} copy(f32[2,64,512]{2,1,0:T(8,128)} %shard_map.73) | data formatting | bytes 524288
where the time goes:
time: 33.6 us; the launch traced here: 33.4 us
  Pallas kernels  31.8 us (95%)
  local copies, waits for them, and re-layouts  1.67 us (5%)
    pallas_call x1, Pallas kernels, shards(): pl.pallas_call(functools.partial(kernel, 'row', count), out_shape=jax.Sha...  31.8 us
    unnamed x1, local copies, waits for them, and re-layouts  1.67 us

commit v1 on v0

--- a/solution.py
+++ b/solution.py
@@ -274,9 +274,14 @@
     block_one[...] = gather(1)
 
     complete_zero()
-    product[...] = complex_product(solution_zero[...], high.at[1], low.at[1])
+
+    def update_half(first):
+        rows = pl.ds(first, pairs)
+        product[rows] = complex_product(solution_zero[rows], high.at[1], low.at[1])
+
+    update_half((1 - core) * pairs)
     pair_copy().start()
-    deal_chip(middle)
+    update_half(core * pairs)
     pair_copy().wait_recv()
     mine = product[pl.ds(core * pairs, pairs)]
     theirs = jnp.full(mine.shape, block_at(sibling), jnp.int32) == 1
@@ -284,7 +289,7 @@
     each_chip(lambda other: hand_back(other).start())
     returned[chip] = merged[chip]
 
-    @pl.loop(middle + 1, pairs - 1)
+    @pl.loop(middle, pairs - 1)
     def _(step):
         deal_chip(step)
 

time: 33.6 us -> 33.6 us (level)
  no operation moved by 1% of the time
where the time goes in v1:
time: 33.6 us; the launch traced here: 33.5 us
  Pallas kernels  31.8 us (95%)
  local copies, waits for them, and re-layouts  1.67 us (5%)
    pallas_call x1, Pallas kernels, shards(): pl.pallas_call(functools.partial(kernel, 'row', count), out_shape=jax.Sha...  31.8 us
    unnamed x1, local copies, waits for them, and re-layouts  1.67 us

profile of v1, /device:TPU:0, one launch (start us, length us, event | category | flops | bytes accessed | tf_op | source)
XLA Modules:
  0.0 33.5 jit_solution(16198293523132998419)
XLA Ops:
  0.0 31.8 %shard_map.73 = f32[2,64,512]{2,1,0:T(8,128)} custom-call(s32[16]{0:T(128)} %owners_in.1, s32[64,128]{1,0:T(8,128)} %bitcast.1, f32[2,4,8192]{2,1,0:T(4,128)} %rhs_in.1, f32[2,512,512]{2,1,0:T(8,128)} %panel_first.1, f32[2,512,512]{2,1,0:T(8,128)} %panel_second.1, f32[2,512,512]{2,1,0:T(8,128)} %inverse_first.1, f32[2,512,512]{2,1,0:T(8,128)} %inverse_second.1), custom_call_target="tpu_custom_call" | custom-call | flops 4000000000 | bytes 9000000 | tf_op jit(solution)/shard_map/pallas_call | solution.py:354
  31.8 1.7 %copy.9 = f32[2,64,512]{2,1,0:T(8,128)} copy(f32[2,64,512]{2,1,0:T(8,128)} %shard_map.73) | data formatting | bytes 524288
